TPU v7x, 32 devices: a whole 2x2x4 slice. The times are simulated.
32 devices in a mesh: dp: 16 (over z, x, core), mp: 2 (over y).
Axes of the slice: x: 2, y: 2, z: 4, core: 2. Of those that a mesh axis runs over, the one named last changes fastest.
Arguments:
- tokens: bfloat16 [16, 1089, 768], P('dp'), may hold values from -6 to 6
- cotangent: bfloat16 [16, 1089, 768], P('dp'), may hold values from -6 to 6
- long_flag: int32 [16], P('dp'), may hold values from 0 to 1, as said below
- token_mask: int32 [16, 1089], P('dp'), may hold values from 0 to 1, as said below
- bucket_line: int32 [16, 1089, 1089], P('dp'), may hold values from 0 to 31
- bucket_across: int32 [16, 1089, 1089], P('dp'), may hold values from 0 to 63
- bucket_down: int32 [16, 1089, 1089], P('dp'), may hold values from 0 to 63
- project_weight: bfloat16 [3, 768, 768], P(None, None, 'mp'), may hold values from -0.21875 to 0.21875
- project_bias: bfloat16 [2, 768], P(None, 'mp'), may hold values from -4 to 4
- table_line: bfloat16 [32, 12], P(None, 'mp'), may hold values from -6 to 6
- table_across: bfloat16 [64, 12], P(None, 'mp'), may hold values from -6 to 6
- table_down: bfloat16 [64, 12], P(None, 'mp'), may hold values from -6 to 6
- output_weight: bfloat16 [768, 768], P('mp'), may hold values from -1.75 to 1.75
- output_bias: bfloat16 [768], replicated, may hold values from -4 to 4
- first_gain: float32 [768], replicated, may hold values from 0.5 to 1.5
- first_shift: float32 [768], replicated, may hold values from -4 to 4
- expand_weight: bfloat16 [768, 3072], P(None, 'mp'), may hold values from -0.21875 to 0.21875
- expand_bias: bfloat16 [3072], P('mp'), may hold values from -4 to 4
- reduce_weight: bfloat16 [3072, 768], P('mp'), may hold values from -0.109375 to 0.109375
- reduce_bias: bfloat16 [768], replicated, may hold values from -4 to 4
- second_gain: float32 [768], replicated, may hold values from 0.5 to 1.5
- second_shift: float32 [768], replicated, may hold values from -4 to 4
Outputs:
- layer_out: bfloat16 [16, 1089, 768], P('dp')
- input_grad: float32 [16, 1089, 768], P('dp', None, 'mp')
- project_weight_grad: float32 [3, 768, 768], P(None, None, 'mp')
- project_bias_grad: float32 [2, 768], P(None, 'mp')
- table_line_grad: float32 [32, 12], P(None, 'mp')
- table_across_grad: float32 [64, 12], P(None, 'mp')
- table_down_grad: float32 [64, 12], P(None, 'mp')
- output_weight_grad: float32 [768, 768], P('mp')
- output_bias_grad: float32 [768], replicated
- first_gain_grad: float32 [768], P('mp')
- first_shift_grad: float32 [768], P('mp')
- expand_weight_grad: float32 [768, 3072], P(None, 'mp')
- expand_bias_grad: float32 [3072], P('mp')
- reduce_weight_grad: float32 [3072, 768], P('mp')
- reduce_bias_grad: float32 [768], replicated
- second_gain_grad: float32 [768], replicated
- second_shift_grad: float32 [768], replicated
Inputs may be any that keep to these rules, and one draw needn't show every extreme that they name: `long_flag`: 1 marks an item of the long bucket (1089 rows), 0 one of the short bucket (709 rows); both kinds occur. `token_mask`: 1 on an item's first rows and 0 after them; an item of the long bucket has more than 709 ones; an item of the short bucket has 532 ones or more, and its ones may run past row 709; some item of each bucket has ones on all 1089 rows.
All inputs are finite; a program needn't handle non-finite values.
Results may differ from a plain program's by a relative error of at most 0.014.
Values may be sent and summed in bfloat16 or wider, within the bound.
A program may use at most 256 MiB of HBM per device.

v0:
```python
from functools import partial

import jax
import jax.numpy as jnp
from jax import lax
from jax.sharding import PartitionSpec as P

LONG = 1089
SHORT = 709


large_negative = -1000000000.0
norm_epsilon = 1e-05


def one_hot(index_block, level_count):
    levels = jnp.arange(level_count, dtype=jnp.int32)
    return (index_block[:, :, None, :] == levels[None, None, :, None]).astype(jnp.bfloat16)


def bias_lookup(bucket_line, bucket_across, bucket_down, table_line, table_across, table_down):
    item_count, row_count, key_count = bucket_line.shape
    head_count = table_line.shape[1]
    block_rows = row_count // 3

    def fill(block_index, position_bias):
        row_start = block_index * block_rows
        summed = jnp.zeros((item_count, head_count, block_rows, key_count), jnp.float32)
        for index_rows, lookup in (
            (bucket_line, table_line),
            (bucket_across, table_across),
            (bucket_down, table_down),
        ):
            index_block = lax.dynamic_slice_in_dim(index_rows, row_start, block_rows, 1)
            summed = summed + jnp.einsum(
                "kh,brkj->bhrj",
                lookup,
                one_hot(index_block, lookup.shape[0]),
                preferred_element_type=jnp.float32,
            )
        return lax.dynamic_update_slice_in_dim(position_bias, summed, row_start, 2)

    empty = jnp.zeros((item_count, head_count, row_count, key_count), jnp.float32)
    return lax.fori_loop(0, 3, fill, empty)


def table_grads(grad_scores, bucket_line, bucket_across, bucket_down, line_count, plane_count):
    head_count = grad_scores.shape[1]
    row_count = grad_scores.shape[2]
    block_rows = row_count // 3

    def accumulate(block_index, sums):
        row_start = block_index * block_rows
        grad_block = lax.dynamic_slice_in_dim(grad_scores, row_start, block_rows, 2)
        line_sum, across_sum, down_sum = sums
        line_block = lax.dynamic_slice_in_dim(bucket_line, row_start, block_rows, 1)
        across_block = lax.dynamic_slice_in_dim(bucket_across, row_start, block_rows, 1)
        down_block = lax.dynamic_slice_in_dim(bucket_down, row_start, block_rows, 1)
        line_sum = line_sum + jnp.einsum(
            "brkj,bhrj->kh",
            one_hot(line_block, line_count),
            grad_block,
            preferred_element_type=jnp.float32,
        )
        across_sum = across_sum + jnp.einsum(
            "brkj,bhrj->kh",
            one_hot(across_block, plane_count),
            grad_block,
            preferred_element_type=jnp.float32,
        )
        down_sum = down_sum + jnp.einsum(
            "brkj,bhrj->kh",
            one_hot(down_block, plane_count),
            grad_block,
            preferred_element_type=jnp.float32,
        )
        return (line_sum, across_sum, down_sum)

    start_sums = (
        jnp.zeros((line_count, head_count), jnp.float32),
        jnp.zeros((plane_count, head_count), jnp.float32),
        jnp.zeros((plane_count, head_count), jnp.float32),
    )
    return lax.fori_loop(0, 3, accumulate, start_sums)


def score_rows(query_heads, key_heads, position_bias, valid):
    raw_scores = (
        jnp.einsum("bihd,bjhd->bhij", query_heads, key_heads, preferred_element_type=jnp.float32)
        * 0.125
        + position_bias
    )
    return jnp.where(valid[:, None, None, :] > 0, raw_scores, large_negative)


def norm_parts(values, gain_vector, shift_vector):
    average = jnp.mean(values, axis=-1, keepdims=True)
    centered = values - average
    variance = jnp.mean(centered * centered, axis=-1, keepdims=True)
    inverse = lax.rsqrt(variance + norm_epsilon)
    normal_hat = centered * inverse
    return (normal_hat * gain_vector + shift_vector, normal_hat, inverse)


def norm_back(grad_hat, normal_hat, inverse):
    first_mean = jnp.mean(grad_hat, axis=-1, keepdims=True)
    cross_mean = jnp.mean(grad_hat * normal_hat, axis=-1, keepdims=True)
    return inverse * (grad_hat - first_mean - normal_hat * cross_mean)


def feed_total(
    expand_weight_grad,
    expand_bias_grad,
    reduce_weight_grad,
    reduce_bias_grad,
    second_gain_grad,
    second_shift_grad,
):
    return (
        expand_weight_grad,
        expand_bias_grad,
        reduce_weight_grad,
        reduce_bias_grad,
        second_gain_grad,
        second_shift_grad,
    )


def final_total(attention_part, feed_part):
    (
        project_weight_grad,
        project_bias_grad,
        table_line_grad,
        table_across_grad,
        table_down_grad,
        output_weight_grad,
        output_bias_grad,
        first_gain_grad,
        first_shift_grad,
    ) = attention_part
    (
        expand_weight_grad,
        expand_bias_grad,
        reduce_weight_grad,
        reduce_bias_grad,
        second_gain_grad,
        second_shift_grad,
    ) = feed_part
    (
        project_weight_grad,
        project_bias_grad,
        table_line_grad,
        table_across_grad,
        table_down_grad,
        output_weight_grad,
        output_bias_grad,
        first_gain_grad,
        first_shift_grad,
        expand_weight_grad,
        expand_bias_grad,
        reduce_weight_grad,
        reduce_bias_grad,
        second_gain_grad,
        second_shift_grad,
    ) = lax.psum(
        (
            project_weight_grad,
            project_bias_grad,
            table_line_grad,
            table_across_grad,
            table_down_grad,
            output_weight_grad,
            output_bias_grad,
            first_gain_grad,
            first_shift_grad,
            expand_weight_grad,
            expand_bias_grad,
            reduce_weight_grad,
            reduce_bias_grad,
            second_gain_grad,
            second_shift_grad,
        ),
        "dp",
    )
    return (
        project_weight_grad,
        project_bias_grad,
        table_line_grad,
        table_across_grad,
        table_down_grad,
        output_weight_grad,
        output_bias_grad,
        first_gain_grad,
        first_shift_grad,
        expand_weight_grad,
        expand_bias_grad,
        reduce_weight_grad,
        reduce_bias_grad,
        second_gain_grad,
        second_shift_grad,
    )


def heads_layer(tokens, cotangent, valid, buckets, weights):
    bucket_line, bucket_across, bucket_down = buckets
    (
        project_weight,
        project_bias,
        table_line,
        table_across,
        table_down,
        output_weight,
        output_bias,
        first_gain,
        first_shift,
        expand_weight,
        expand_bias,
        reduce_weight,
        reduce_bias,
        second_gain,
        second_shift,
    ) = weights
    item_count, row_count, full_width = tokens.shape
    local_width = project_weight.shape[2]
    head_count = table_line.shape[1]
    head_width = local_width // head_count
    head_shape = (item_count, row_count, head_count, head_width)
    projected = jnp.einsum(
        "bld,kde->kble", tokens, project_weight, preferred_element_type=jnp.float32
    )
    queries = (projected[0] + project_bias[0].astype(jnp.float32)).astype(jnp.bfloat16)
    key_rows = projected[1].astype(jnp.bfloat16)
    value_rows = (projected[2] + project_bias[1].astype(jnp.float32)).astype(jnp.bfloat16)
    query_heads = queries.reshape(head_shape)
    key_heads = key_rows.reshape(head_shape)
    value_heads = value_rows.reshape(head_shape)
    position_bias = bias_lookup(
        bucket_line, bucket_across, bucket_down, table_line, table_across, table_down
    )
    scores = score_rows(query_heads, key_heads, position_bias, valid)
    topmost = jnp.max(scores, axis=-1, keepdims=True)
    exponent = jnp.exp(scores - topmost)
    summed = jnp.sum(exponent, axis=-1, keepdims=True)
    attention = exponent / summed
    log_total = topmost + jnp.log(summed)
    context = jnp.einsum(
        "bhij,bjhd->bihd",
        attention.astype(jnp.bfloat16),
        value_heads,
        preferred_element_type=jnp.float32,
    )
    context = context.reshape(item_count, row_count, local_width).astype(jnp.bfloat16)
    attended_part = jnp.einsum(
        "bie,ef->bif", context, output_weight, preferred_element_type=jnp.float32
    )
    attended = lax.psum(attended_part, "mp") + output_bias.astype(jnp.float32)
    first_norm, first_hat, first_inverse = norm_parts(
        tokens.astype(jnp.float32) + attended, first_gain, first_shift
    )
    expand_input = first_norm.astype(jnp.bfloat16)
    before = jnp.einsum(
        "bld,df->blf", expand_input, expand_weight, preferred_element_type=jnp.float32
    )
    before = before + expand_bias.astype(jnp.float32)
    activated, gelu_back = jax.vjp(partial(jax.nn.gelu, approximate=False), before)
    activated_low = activated.astype(jnp.bfloat16)
    reduced_part = jnp.einsum(
        "blf,fd->bld", activated_low, reduce_weight, preferred_element_type=jnp.float32
    )
    reduced = lax.psum(reduced_part, "mp") + reduce_bias.astype(jnp.float32)
    second_norm, second_hat, second_inverse = norm_parts(
        first_norm + reduced, second_gain, second_shift
    )
    layer_out = (second_norm * valid[:, :, None]).astype(jnp.bfloat16)
    grad_out = cotangent.astype(jnp.float32) * valid[:, :, None]
    second_gain_grad = jnp.sum(grad_out * second_hat, axis=(0, 1))
    second_shift_grad = jnp.sum(grad_out, axis=(0, 1))
    grad_mixed = norm_back(grad_out * second_gain, second_hat, second_inverse)
    grad_reduced = grad_mixed.astype(jnp.bfloat16)
    reduce_bias_grad = jnp.sum(grad_reduced, axis=(0, 1), dtype=jnp.float32)
    reduce_weight_grad = jnp.einsum(
        "blf,bld->fd", activated_low, grad_reduced, preferred_element_type=jnp.float32
    )
    grad_active = jnp.einsum(
        "bld,fd->blf", grad_reduced, reduce_weight, preferred_element_type=jnp.float32
    )
    grad_before = gelu_back(grad_active)[0].astype(jnp.bfloat16)
    expand_bias_grad = jnp.sum(grad_before, axis=(0, 1), dtype=jnp.float32)
    expand_weight_grad = jnp.einsum(
        "bld,blf->df", expand_input, grad_before, preferred_element_type=jnp.float32
    )
    feed_part = feed_total(
        expand_weight_grad,
        expand_bias_grad,
        reduce_weight_grad,
        reduce_bias_grad,
        second_gain_grad,
        second_shift_grad,
    )
    hidden_part = jnp.einsum(
        "blf,df->bld", grad_before, expand_weight, preferred_element_type=jnp.float32
    )
    hidden_share = lax.psum_scatter(hidden_part, "mp", scatter_dimension=2, tiled=True)
    row_start = lax.axis_index("mp") * local_width
    grad_first = lax.dynamic_slice_in_dim(grad_mixed, row_start, local_width, 2) + hidden_share
    first_hat_own = lax.dynamic_slice_in_dim(first_hat, row_start, local_width, 2)
    gain_own = lax.dynamic_slice_in_dim(first_gain, row_start, local_width, 0)
    grad_hat = grad_first * gain_own
    first_gain_grad = jnp.sum(grad_first * first_hat_own, axis=(0, 1))
    first_shift_grad = jnp.sum(grad_first, axis=(0, 1))
    hat_total, hat_cross = lax.psum(
        (jnp.sum(grad_hat, axis=-1), jnp.sum(grad_hat * first_hat_own, axis=-1)), "mp"
    )
    grad_inner = first_inverse * (
        grad_hat
        - hat_total[:, :, None] / full_width
        - first_hat_own * (hat_cross[:, :, None] / full_width)
    )
    grad_attended = lax.all_gather(grad_inner.astype(jnp.bfloat16), "mp", axis=2, tiled=True)
    output_bias_grad = jnp.sum(grad_attended, axis=(0, 1), dtype=jnp.float32)
    output_weight_grad = jnp.einsum(
        "bie,bif->ef", context, grad_attended, preferred_element_type=jnp.float32
    )
    grad_context = jnp.einsum(
        "bif,ef->bie", grad_attended, output_weight, preferred_element_type=jnp.float32
    )
    grad_context = grad_context.astype(jnp.bfloat16).reshape(head_shape)
    scores = score_rows(query_heads, key_heads, position_bias, valid)
    attention = jnp.exp(scores - log_total)
    attention_low = attention.astype(jnp.bfloat16)
    grad_attention = jnp.einsum(
        "bihd,bjhd->bhij", grad_context, value_heads, preferred_element_type=jnp.float32
    )
    inner_total = jnp.sum(attention * grad_attention, axis=-1, keepdims=True)
    grad_scores = (attention * (grad_attention - inner_total)).astype(jnp.bfloat16)
    table_line_grad, table_across_grad, table_down_grad = table_grads(
        grad_scores,
        bucket_line,
        bucket_across,
        bucket_down,
        table_line.shape[0],
        table_across.shape[0],
    )
    flat_shape = (item_count, row_count, local_width)
    grad_query = (
        (
            jnp.einsum(
                "bhij,bjhd->bihd", grad_scores, key_heads, preferred_element_type=jnp.float32
            )
            * 0.125
        )
        .astype(jnp.bfloat16)
        .reshape(flat_shape)
    )
    grad_key = (
        (
            jnp.einsum(
                "bhij,bihd->bjhd", grad_scores, query_heads, preferred_element_type=jnp.float32
            )
            * 0.125
        )
        .astype(jnp.bfloat16)
        .reshape(flat_shape)
    )
    grad_value = (
        jnp.einsum(
            "bhij,bihd->bjhd", attention_low, grad_context, preferred_element_type=jnp.float32
        )
        .astype(jnp.bfloat16)
        .reshape(flat_shape)
    )
    project_bias_grad = jnp.stack(
        [
            jnp.sum(grad_query, axis=(0, 1), dtype=jnp.float32),
            jnp.sum(grad_value, axis=(0, 1), dtype=jnp.float32),
        ]
    )
    stacked = jnp.stack([grad_query, grad_key, grad_value])
    project_weight_grad = jnp.einsum(
        "bld,kble->kde", tokens, stacked, preferred_element_type=jnp.float32
    )
    input_part = jnp.einsum(
        "kble,kde->bld", stacked, project_weight, preferred_element_type=jnp.float32
    )
    input_grad = (
        lax.psum_scatter(
            input_part.astype(jnp.bfloat16), "mp", scatter_dimension=2, tiled=True
        ).astype(jnp.float32)
        + grad_inner
    )
    attention_part = (
        project_weight_grad,
        project_bias_grad,
        table_line_grad,
        table_across_grad,
        table_down_grad,
        output_weight_grad,
        output_bias_grad,
        first_gain_grad,
        first_shift_grad,
    )
    return (layer_out, input_grad, attention_part, feed_part)


def per_device(
    tokens,
    cotangent,
    long_flag,
    token_mask,
    bucket_line,
    bucket_across,
    bucket_down,
    project_weight,
    project_bias,
    table_line,
    table_across,
    table_down,
    output_weight,
    output_bias,
    first_gain,
    first_shift,
    expand_weight,
    expand_bias,
    reduce_weight,
    reduce_bias,
    second_gain,
    second_shift,
):
    positions = jnp.arange(tokens.shape[1], dtype=jnp.int32)
    limits = jnp.where(long_flag > 0, LONG, SHORT).astype(jnp.int32)
    valid = ((token_mask > 0) & (positions[None, :] < limits[:, None])).astype(jnp.float32)
    buckets = (bucket_line, bucket_across, bucket_down)
    weights = (
        project_weight,
        project_bias,
        table_line,
        table_across,
        table_down,
        output_weight,
        output_bias,
        first_gain,
        first_shift,
        expand_weight,
        expand_bias,
        reduce_weight,
        reduce_bias,
        second_gain,
        second_shift,
    )
    layer_out, input_grad, attention_part, feed_part = heads_layer(
        tokens, cotangent, valid, buckets, weights
    )
    return (layer_out, input_grad) + final_total(attention_part, feed_part)


def solution(mesh):
    placed = (
        P("dp", None, None),
        P("dp", None, None),
        P("dp"),
        P("dp", None),
        P("dp", None, None),
        P("dp", None, None),
        P("dp", None, None),
        P(None, None, "mp"),
        P(None, "mp"),
        P(None, "mp"),
        P(None, "mp"),
        P(None, "mp"),
        P("mp", None),
        P(),
        P(),
        P(),
        P(None, "mp"),
        P("mp"),
        P("mp", None),
        P(),
        P(),
        P(),
    )
    return jax.shard_map(
        per_device,
        mesh=mesh,
        in_specs=placed,
        out_specs=(
            P("dp", None, None),
            P("dp", None, "mp"),
            P(None, None, "mp"),
            P(None, "mp"),
            P(None, "mp"),
            P(None, "mp"),
            P(None, "mp"),
            P("mp", None),
            P(),
            P("mp"),
            P("mp"),
            P(None, "mp"),
            P("mp"),
            P("mp", None),
            P(),
            P(),
            P(),
        ),
        check_vma=False,
    )
```

profile of v0, /device:TPU:0, one launch (start us, length us, event | category | flops | bytes accessed | tf_op | source)
XLA Modules:
  0.0 1272.4 jit_solution(6401770787973455738)
XLA Ops:
  36.8 380.6 %while.31 = (s32[]{:T(128)}, f32[1,6,1089,1089]{2,3,1,0:T(8,128)}, s32[1,1089,1089]{2,0,1:T(1,128)}, bf16[32,6]{0,1:T(8,128)(2,1)S(1)}, s32[1,1089,1089]{2,0,1:T...) while((s32[]{:T(128)}, f32[1,6,1089,1089]{2,3,1,0:T(8,128)}, ...), condition=%wide.region_1.2_spmd, body=%wide.region_0.1_spmd.sunk | while | flops 826982272 | bytes 109106824 | solution.py:44
  44.3 18.0 %fusion.125 = f32[363,1089,6]{1,2,0:T(8,128)} fusion(s32[363,1089]{1,0:T(8,128)S(1)} %bitcast.230, bf16[64,6]{0,1:T(8,128)(2,1)S(1)} %get-tuple-element.648), kind=kOutput, calls=%fused_computation.2.clone.1 | convolution fusion | flops 328895424 | bytes 11069364 | tf_op jit(solution)/shard_map/while/body/eval_jaxpr/kh,brkj->bhrj/dot_general | solution.py:35
  72.6 21.6 %add_bitcast_fusion.2 = f32[1,6,363,1089]{3,1,2,0:T(8,128)} fusion(f32[363,1089,6]{1,2,0:T(8,128)} %fusion.124, f32[363,1089,6]{1,2,0:T(8,128)} %fusion.125, s32[363,1089]{1,0:T(8,128)S(1)} %bitcast.228, bf16[64,6]{0,1:T(8,128)(2,1)S(1)} %get-tuple-element.650), kind=kOutput, calls=%fused_computation.9.clone.1 | convolution fusion | flops 333639104 | bytes 30044100 | tf_op jit(solution)/shard_map/while/body/eval_jaxpr/kh,brkj->bhrj/dot_general | solution.py:35
  107.4 52.6 %dynamic_update_slice.8 = f32[1,6,1089,1089]{2,3,1,0:T(8,128)} dynamic-update-slice(f32[1,6,1089,1089]{2,3,1,0:T(8,128)} %get-tuple-element.632, f32[1,6,363,1089]{2,3,1,0:T(8,128)} %copy.176, s32[]{:T(128)} %constant.63.clone.1..sunk, s32[]{:T(128)} %constant.63.clone.1..sunk, s32[]{:T(128)S(6)} %select_n.41, s32[]{:T(128)} %constant.63.clone.1..sunk) | dynamic-update-slice | bytes 18974740 | tf_op jit(solution)/shard_map/while/body/eval_jaxpr/dynamic_update_slice | solution.py:41
  195.5 21.6 %add_bitcast_fusion.2 = f32[1,6,363,1089]{3,1,2,0:T(8,128)} fusion(f32[363,1089,6]{1,2,0:T(8,128)} %fusion.124, f32[363,1089,6]{1,2,0:T(8,128)} %fusion.125, s32[363,1089]{1,0:T(8,128)S(1)} %bitcast.228, bf16[64,6]{0,1:T(8,128)(2,1)S(1)} %get-tuple-element.650), kind=kOutput, calls=%fused_computation.9.clone.1 | convolution fusion | flops 333639104 | bytes 30044100 | tf_op jit(solution)/shard_map/while/body/eval_jaxpr/kh,brkj->bhrj/dot_general | solution.py:35
  230.3 58.5 %dynamic_update_slice.8 = f32[1,6,1089,1089]{2,3,1,0:T(8,128)} dynamic-update-slice(f32[1,6,1089,1089]{2,3,1,0:T(8,128)} %get-tuple-element.632, f32[1,6,363,1089]{2,3,1,0:T(8,128)} %copy.176, s32[]{:T(128)} %constant.63.clone.1..sunk, s32[]{:T(128)} %constant.63.clone.1..sunk, s32[]{:T(128)S(6)} %select_n.41, s32[]{:T(128)} %constant.63.clone.1..sunk) | dynamic-update-slice | bytes 18974740 | tf_op jit(solution)/shard_map/while/body/eval_jaxpr/dynamic_update_slice | solution.py:41
  324.3 21.6 %add_bitcast_fusion.2 = f32[1,6,363,1089]{3,1,2,0:T(8,128)} fusion(f32[363,1089,6]{1,2,0:T(8,128)} %fusion.124, f32[363,1089,6]{1,2,0:T(8,128)} %fusion.125, s32[363,1089]{1,0:T(8,128)S(1)} %bitcast.228, bf16[64,6]{0,1:T(8,128)(2,1)S(1)} %get-tuple-element.650), kind=kOutput, calls=%fused_computation.9.clone.1 | convolution fusion | flops 333639104 | bytes 30044100 | tf_op jit(solution)/shard_map/while/body/eval_jaxpr/kh,brkj->bhrj/dot_general | solution.py:35
  359.1 57.9 %dynamic_update_slice.8 = f32[1,6,1089,1089]{2,3,1,0:T(8,128)} dynamic-update-slice(f32[1,6,1089,1089]{2,3,1,0:T(8,128)} %get-tuple-element.632, f32[1,6,363,1089]{2,3,1,0:T(8,128)} %copy.176, s32[]{:T(128)} %constant.63.clone.1..sunk, s32[]{:T(128)} %constant.63.clone.1..sunk, s32[]{:T(128)S(6)} %select_n.41, s32[]{:T(128)} %constant.63.clone.1..sunk) | dynamic-update-slice | bytes 18974740 | tf_op jit(solution)/shard_map/while/body/eval_jaxpr/dynamic_update_slice | solution.py:41
  417.4 23.6 %fusion.94 = (f32[6,1089]{1,0:T(8,128)S(1)}, f32[1,6,1089,1089]{2,3,1,0:T(8,128)}) fusion(f32[1,6,1089,1089]{2,3,1,0:T(8,128)} %get-tuple-element.297, bf16[1089,6,64]{0,2,1:T(8,128)(2,1)S(1)} %bitcast.237, f32[1089,6,64]{0,2,1:T(8,128)} %bitcast.234, f32[6,64]{1,0:T(8,128)S(1)} %copy-done.31, pred[1089]{0:T(1024)(128)(4,1)S(1)} %copy-done.46), kind=kOutput, calls=%fused_computation.162 | convolution fusion | flops 940079232 | bytes 59462024 | tf_op jit(solution)/shard_map/bihd,bjhd->bhij/dot_general | solution.py:89
  470.0 93.3 %all-reduce.7.cloned.1.call-done = f32[1,1089,768]{2,1,0:T(8,128)} async-done(((f32[1,1089,768]{2,1,0:T(8,128)}), f32[1,1089,768]{2,1,0:T(8,128)}) %all-reduce.7.cloned.1.call-update) | async-done | bytes 3345424 | tf_op jit(solution)/shard_map/psum | solution.py:256
  568.9 18.2 %multiply_convert_fusion = (bf16[1089,1536]{1,0:T(8,128)(2,1)S(1)}, f32[1089,1536]{1,0:T(8,128)}, f32[1089,1536]{1,0:T(8,128)}) fusion(f32[1536]{0:T(1024)S(1)} %convert_element_type.204, bf16[768,1536]{1,0:T(8,128)(2,1)S(1)} %copy-done, f32[1,1089,768]{2,1,0:T(8,128)S(1)} %subtract_multiply_fusion.2, f32[768]{0:T(1024)S(1)} %copy-done.30, ...), kind=kOutput, calls=%fused_computation.66 | convolution fusion | flops 2682180864 | bytes 22444032 | tf_op jit(solution)/shard_map/bld,df->blf/dot_general | solution.py:261
  594.3 90.2 %all-reduce.9.cloned.1.call-done = f32[1,1089,768]{2,1,0:T(8,128)} async-done(((f32[1,1089,768]{2,1,0:T(8,128)}), f32[1,1089,768]{2,1,0:T(8,128)}) %all-reduce.9.cloned.1.call-update) | async-done | bytes 3345424 | tf_op jit(solution)/shard_map/psum | solution.py:270
  711.0 46.0 %reduce-scatter.5.cloned.1.call-done = f32[1,1089,384]{2,1,0:T(8,128)} async-done(((f32[1,1089,768]{2,1,0:T(8,128)}), f32[1,1089,384]{2,1,0:T(8,128)}) %reduce-scatter.5.cloned.1.call-update) | async-done | bytes 1672720 | tf_op jit(solution)/shard_map/reduce_scatter | solution.py:303
  768.8 28.6 %all-gather.2.cloned.1.call-done = bf16[1,1089,768]{2,1,0:T(8,128)(2,1)} async-done(((bf16[1,1089,384]{2,1,0:T(8,128)(2,1)}), bf16[1,1089,768]{2,1,0:T(8,128)(2,1)}) %all-gather.2.cloned.1.call-update) | async-done | bytes 1672720 | tf_op jit(solution)/shard_map/all_gather | solution.py:319
  816.3 22.7 %fusion.25 = (f32[6,1089]{1,0:T(8,128)S(1)}, f32[6,1089,1089]{1,2,0:T(8,128)}) fusion(f32[1,6,1089,1089]{2,3,1,0:T(8,128)} %get-tuple-element.501, f32[6,1089]{1,0:T(8,128)S(1)} %log_add_fusion, bf16[1089,6,64]{0,2,1:T(8,128)(2,1)S(1)} %bitcast.240, f32[1089,6,64]{0,2,1:T(8,128)S(1)} %bitcast.242, f32[6,64]{1,0:T(8,128)S(1)} %copy-done.37), kind=kOutput, calls=%fused_computation.46 | convolution fusion | flops 932963712 | bytes 59487072 | tf_op jit(solution)/shard_map/bihd,bjhd->bhij/dot_general | solution.py:331
  838.9 25.5 %fusion.24 = bf16[1,6,1089,1089]{2,3,1,0:T(8,128)(2,1)} fusion(f32[6,1089,1089]{1,2,0:T(8,128)} %get-tuple-element.504, f32[1,6,1089,1089]{2,3,1,0:T(8,128)} %get-tuple-element.501, f32[6,1089]{1,0:T(8,128)S(1)} %get-tuple-element.503, f32[6,1089]{1,0:T(8,128)S(1)} %log_add_fusion), kind=kLoop, calls=%fused_computation.44 | loop fusion | flops 28462104 | bytes 71207536 | tf_op jit(solution)/shard_map/convert_element_type | solution.py:335
  925.5 245.7 %while.32 = (s32[]{:T(128)}, f32[32,6]{0,1:T(8,128)S(1)}, f32[64,6]{0,1:T(8,128)S(1)}, f32[64,6]{0,1:T(8,128)S(1)}, s32[1,1089,1089]{2,0,1:T(1,128)}, /*index=5*...) while((s32[]{:T(128)}, f32[32,6]{0,1:T(8,128)S(1)}, ...), condition=%wide.region_24.25_spmd.clone, body=%wide.region_23.24_spmd.clone.sunk | while | flops 822240512 | bytes 66419532 | solution.py:84
  969.7 20.0 %fusion.128 = f32[64,6]{0,1:T(8,128)S(1)} fusion(bf16[1,6,363,1089]{2,3,1,0:T(8,128)(2,1)S(1)} %constant_dynamic-slice_fusion.14, s32[363,1089]{0,1:T(8,128)S(1)} %bitcast.233, f32[64,6]{0,1:T(8,128)S(1)} %get-tuple-element.670, pred[]{:T(512)S(6)} %compare.3), kind=kOutput, calls=%fused_computation.33.clone.1 | convolution fusion | flops 328896192 | bytes 6327985 | tf_op jit(solution)/shard_map/while/body/eval_jaxpr/brkj,bhrj->kh/dot_general | solution.py:71
  989.8 20.0 %fusion.127 = f32[64,6]{0,1:T(8,128)S(1)} fusion(bf16[1,6,363,1089]{2,3,1,0:T(8,128)(2,1)S(1)} %constant_dynamic-slice_fusion.14, s32[363,1089]{0,1:T(8,128)S(1)} %bitcast.232, f32[64,6]{0,1:T(8,128)S(1)} %get-tuple-element.669, pred[]{:T(512)S(6)} %compare.3), kind=kOutput, calls=%fused_computation.32.clone.1 | convolution fusion | flops 328896192 | bytes 6327985 | tf_op jit(solution)/shard_map/while/body/eval_jaxpr/brkj,bhrj->kh/dot_general | solution.py:65
  1045.8 20.0 %fusion.128 = f32[64,6]{0,1:T(8,128)S(1)} fusion(bf16[1,6,363,1089]{2,3,1,0:T(8,128)(2,1)S(1)} %constant_dynamic-slice_fusion.14, s32[363,1089]{0,1:T(8,128)S(1)} %bitcast.233, f32[64,6]{0,1:T(8,128)S(1)} %get-tuple-element.670, pred[]{:T(512)S(6)} %compare.3), kind=kOutput, calls=%fused_computation.33.clone.1 | convolution fusion | flops 328896192 | bytes 6327985 | tf_op jit(solution)/shard_map/while/body/eval_jaxpr/brkj,bhrj->kh/dot_general | solution.py:71
  1065.9 20.0 %fusion.127 = f32[64,6]{0,1:T(8,128)S(1)} fusion(bf16[1,6,363,1089]{2,3,1,0:T(8,128)(2,1)S(1)} %constant_dynamic-slice_fusion.14, s32[363,1089]{0,1:T(8,128)S(1)} %bitcast.232, f32[64,6]{0,1:T(8,128)S(1)} %get-tuple-element.669, pred[]{:T(512)S(6)} %compare.3), kind=kOutput, calls=%fused_computation.32.clone.1 | convolution fusion | flops 328896192 | bytes 6327985 | tf_op jit(solution)/shard_map/while/body/eval_jaxpr/brkj,bhrj->kh/dot_general | solution.py:65
  1121.7 20.0 %fusion.128 = f32[64,6]{0,1:T(8,128)S(1)} fusion(bf16[1,6,363,1089]{2,3,1,0:T(8,128)(2,1)S(1)} %constant_dynamic-slice_fusion.14, s32[363,1089]{0,1:T(8,128)S(1)} %bitcast.233, f32[64,6]{0,1:T(8,128)S(1)} %get-tuple-element.670, pred[]{:T(512)S(6)} %compare.3), kind=kOutput, calls=%fused_computation.33.clone.1 | convolution fusion | flops 328896192 | bytes 6327985 | tf_op jit(solution)/shard_map/while/body/eval_jaxpr/brkj,bhrj->kh/dot_general | solution.py:71
  1141.7 20.0 %fusion.127 = f32[64,6]{0,1:T(8,128)S(1)} fusion(bf16[1,6,363,1089]{2,3,1,0:T(8,128)(2,1)S(1)} %constant_dynamic-slice_fusion.14, s32[363,1089]{0,1:T(8,128)S(1)} %bitcast.232, f32[64,6]{0,1:T(8,128)S(1)} %get-tuple-element.669, pred[]{:T(512)S(6)} %compare.3), kind=kOutput, calls=%fused_computation.32.clone.1 | convolution fusion | flops 328896192 | bytes 6327985 | tf_op jit(solution)/shard_map/while/body/eval_jaxpr/brkj,bhrj->kh/dot_general | solution.py:65
  1173.4 62.0 %all-reduce = (f32[2,384]{1,0:T(2,128)}, f32[32,6]{0,1:T(8,128)}, f32[64,6]{0,1:T(8,128)}, f32[64,6]{0,1:T(8,128)}, f32[768]{0:T(1024)}, /*index=5*/f32[384]{0:T...) all-reduce(f32[2,384]{1,0:T(2,128)S(1)} %pad_maximum_fusion, ...), channel_id=1, replica_groups=mesh['dp'=16,'mp'=2] {'dp'}, use_global_device_ids=true, to_apply=%region_22.23 | all-reduce | flops 7104 | bytes 56832 | tf_op jit(solution)/shard_map/psum | solution.py:165
  (290 shorter events, 455.5 us)
Async XLA Ops:
  7.2 561.7 %copy-start = (bf16[768,1536]{1,0:T(8,128)(2,1)S(1)}, bf16[768,1536]{1,0:T(8,128)(2,1)}, u32[]{:S(2)}) copy-start(bf16[768,1536]{1,0:T(8,128)(2,1)} %param.42) | copy-start | bytes 7077892
  7.2 556.1 %all-reduce.7.cloned.1.call-start = ((), (), s32[]{:S(2)}) async-start(), calls=%async_computation.2 | async-start | bytes 6733824 | tf_op jit(solution)/shard_map/psum | solution.py:256
  36.8 380.7 %copy-start.13 = (bf16[1,1,1089,384]{2,3,1,0:T(8,128)(2,1)S(1)}, bf16[1,1,1089,384]{2,3,1,0:T(8,128)(2,1)}, u32[]{:S(2)}) copy-start(bf16[1,1,1089,384]{2,3,1,0:T(8,128)(2,1)} %copy.85) | copy-start | bytes 2509060
  36.8 380.7 %copy-start.31 = (f32[6,64]{1,0:T(8,128)S(1)}, f32[6,64]{1,0:T(8,128)}, u32[]{:S(2)}) copy-start(f32[6,64]{1,0:T(8,128)} %reshape.539) | copy-start | bytes 4612
  36.8 380.7 %copy-start.46 = (pred[1089]{0:T(1024)(128)(4,1)S(1)}, pred[1089]{0:T(1024)(128)(4,1)}, u32[]{:S(2)}) copy-start(pred[1089]{0:T(1024)(128)(4,1)} %broadcast_compare_fusion) | copy-start | bytes 3271
  469.9 214.6 %all-reduce.9.cloned.1.call-start = ((), (), s32[]{:S(2)}) async-start(), calls=%async_computation.3 | async-start | bytes 6733824 | tf_op jit(solution)/shard_map/psum | solution.py:270
  568.2 197.6 %copy-start.33 = (f32[1089]{0:T(1024)}, f32[1089]{0:T(1024)S(1)}, u32[]{:S(2)}) copy-start(f32[1089]{0:T(1024)S(1)} %add_rsqrt_fusion.1) | copy-start | bytes 13072
  593.6 163.4 %reduce-scatter.5.cloned.1.call-start = ((), (), s32[]{:S(2)}) async-start(), calls=%async_computation.4 | async-start | bytes 5050368 | tf_op jit(solution)/shard_map/reduce_scatter | solution.py:303
  710.9 86.5 %all-gather.2.cloned.1.call-start = ((), (), s32[]{:S(2)}) async-start(), calls=%async_computation.5 | async-start | bytes 2525184 | tf_op jit(solution)/shard_map/all_gather | solution.py:319
  768.7 466.7 %reduce-scatter.7.cloned.1.call-start = ((), (), s32[]{:S(2)}) async-start(), calls=%async_computation.6 | async-start | bytes 2654208
  904.6 346.6 %all-reduce.11.cloned.1.call-start = ((), (), s32[]{:S(2)}) async-start(), calls=%async_computation.7 | async-start | bytes 28311552 | tf_op jit(solution)/shard_map/psum | solution.py:165
  925.4 245.8 %copy-start.52 = (f32[6,64]{1,0:T(8,128)S(1)}, f32[6,64]{1,0:T(8,128)}, u32[]{:S(2)}) copy-start(f32[6,64]{1,0:T(8,128)} %get-tuple-element.505) | copy-start | bytes 4612
  925.4 245.9 %copy-start.48 = (f32[6,64]{1,0:T(8,128)S(1)}, f32[6,64]{1,0:T(8,128)}, u32[]{:S(2)}) copy-start(f32[6,64]{1,0:T(8,128)} %get-tuple-element.507) | copy-start | bytes 4612
  925.5 247.9 %copy-start.49 = (f32[768]{0:T(1024)S(1)}, f32[768]{0:T(1024)}, u32[]{:S(2)}) copy-start(f32[768]{0:T(1024)} %get-tuple-element.427) | copy-start | bytes 9220
  925.5 247.9 %copy-start.50 = (f32[768]{0:T(1024)S(1)}, f32[768]{0:T(1024)}, u32[]{:S(2)}) copy-start(f32[768]{0:T(1024)} %get-tuple-element.432) | copy-start | bytes 9220
  925.5 247.9 %copy-start.51 = (f32[768]{0:T(1024)S(1)}, f32[768]{0:T(1024)}, u32[]{:S(2)}) copy-start(f32[768]{0:T(1024)} %get-tuple-element.486) | copy-start | bytes 9220
  925.5 247.9 %copy-start.53 = (f32[384]{0:T(512)S(1)}, f32[384]{0:T(512)}, u32[]{:S(2)}) copy-start(f32[384]{0:T(512)} %get-tuple-element.429) | copy-start | bytes 4612
  925.5 247.9 %copy-start.54 = (f32[384]{0:T(512)S(1)}, f32[384]{0:T(512)}, u32[]{:S(2)}) copy-start(f32[384]{0:T(512)} %get-tuple-element.434) | copy-start | bytes 4612
  925.5 247.9 %copy-start.55 = (f32[1536]{0:T(1024)S(1)}, f32[1536]{0:T(1024)}, u32[]{:S(2)}) copy-start(f32[1536]{0:T(1024)} %get-tuple-element.509) | copy-start | bytes 18436
  1171.4 71.8 %copy-start.12 = (f32[1,1089,384]{2,1,0:T(8,128)S(1)}, f32[1,1089,384]{2,1,0:T(8,128)}, u32[]{:S(2)}) copy-start(f32[1,1089,384]{2,1,0:T(8,128)} %copy-done.11) | copy-start | bytes 5018116
  1171.4 71.8 %copy-start.34 = (f32[1089]{0:T(1024)S(1)}, f32[1089]{0:T(1024)}, u32[]{:S(2)}) copy-start(f32[1089]{0:T(1024)} %copy-done.33) | copy-start | bytes 13072
  1171.4 71.8 %copy-start.39 = (f32[1089]{0:T(1024)S(1)}, f32[1089]{0:T(1024)}, u32[]{:S(2)}) copy-start(f32[1089]{0:T(1024)} %copy-done.38) | copy-start | bytes 13072
  1171.4 71.8 %copy-start.41 = (f32[1089]{0:T(1024)S(1)}, f32[1089]{0:T(1024)}, u32[]{:S(2)}) copy-start(f32[1089]{0:T(1024)} %copy-done.40) | copy-start | bytes 13072
  1171.5 71.8 %copy-start.45 = (f32[384]{0:T(512)S(1)}, f32[384]{0:T(512)}, u32[]{:S(2)}) copy-start(f32[384]{0:T(512)} %copy-done.44) | copy-start | bytes 4612
  (61 other events, 633.2 us)
Sparse Core Ops, SparseCore 0:
  470.0 93.2 all-reduce.6
  593.7 90.7 all-reduce.8
  711.0 45.9 reduce-scatter.4
  768.9 28.4 all-gather.1
  904.7 28.2 reduce-scatter.6
  939.2 258.9 all-reduce.10
where the time goes:
time: 1280 us; the launch traced here: 1270 us
  matrix products  462 us (36%)
  local copies, waits for them, and re-layouts  386 us (30%)
  waiting for transfers between devices  258 us (20%)
  blocking collectives  67.1 us (5%)
  other arithmetic  64.3 us (5%)
  loops' own time  18.7 us (1%)
  between operations  15.9 us (1%)
    dynamic_update_slice x6, local copies, waits for them, and re-layouts, fill(): return lax.dynamic_update_slice_in_dim(position_bias, summed, row_start, 2)  208 us
    dot_general x9, matrix products, fill(): jnp.einsum('kh,brkj->bhrj', lookup, one_hot(index_block, lookup.shape[0])...  150 us
    psum x1, waiting for transfers between devices, heads_layer(): attended = lax.psum(attended_part, 'mp') + output_bias.astype(jnp.float32)  93.3 us
    psum x1, waiting for transfers between devices, heads_layer(): reduced = lax.psum(reduced_part, 'mp') + reduce_bias.astype(jnp.float32)  90.2 us
    psum x1, blocking collectives, final_total(): lax.psum((project_weight_grad, project_bias_grad, table_line_grad, table_...  62 us
    dot_general x3, matrix products, accumulate(): jnp.einsum('brkj,bhrj->kh', one_hot(across_block, plane_count), grad_bloc...  60.1 us
    dot_general x3, matrix products, accumulate(): jnp.einsum('brkj,bhrj->kh', one_hot(down_block, plane_count), grad_block,...  60.1 us
    unnamed x149, local copies, waits for them, and re-layouts  47 us
  transfers between devices with their start and end apart: 6, of which 4 were waited for; matrix products, arithmetic and copies ran while one was open for 21% of the time, Pallas kernels for 0%

commit v1 on v0

v1 whole, which is shorter than its diff:
```python
from functools import partial

import jax
import jax.numpy as jnp
from jax import lax
from jax.experimental import pallas as pl
from jax.experimental.pallas import tpu as pltpu
from jax.sharding import PartitionSpec as P

LONG = 1089
SHORT = 709
HEAD = 64
LANES = 128
STRIP = 16
BLOCK_ROWS = 224

large_negative = -1000000000.0
norm_epsilon = 1e-05
vmem_limit = 56 * 2**20
bf16 = jnp.bfloat16
f32 = jnp.float32


def round_up(value, step):
    return (value + step - 1) // step * step


def whole_spec(array):
    zeros = (0,) * array.ndim
    return pl.BlockSpec(array.shape, lambda i: zeros)


def dot_f32(left, right):
    return jnp.dot(left, right, preferred_element_type=f32)


def gather_lanes(values, index):
    dims = lax.GatherDimensionNumbers(
        offset_dims=(),
        collapsed_slice_dims=(1,),
        start_index_map=(1,),
        operand_batching_dims=(0,),
        start_indices_batching_dims=(0,),
    )
    return lax.gather(
        values,
        index[..., None],
        dims,
        slice_sizes=(1, 1),
        mode=lax.GatherScatterMode.PROMISE_IN_BOUNDS,
    )


def attend_kernel(
    query_ref,
    key_ref,
    value_ref,
    line_ref,
    across_ref,
    down_ref,
    mask_ref,
    table_ref,
    exp_ref,
    context_ref,
    inverse_ref,
    score_ref,
    *,
    line_count,
    plane_count,
):
    heads, rows, keys = exp_ref.shape
    for h in range(heads):
        pair = slice(h // 2 * LANES, (h // 2 + 1) * LANES)
        score_ref[h] = dot_f32(query_ref[:, pair], key_ref[h])

    def strip(r, carry):
        at = pl.ds(pl.multiple_of(r * STRIP, STRIP), STRIP)
        tops = [None] * heads
        for c in range(keys // LANES):
            cols = slice(c * LANES, (c + 1) * LANES)
            line = line_ref[0, at, cols].astype(jnp.int16) & jnp.int16(line_count - 1)
            across = across_ref[0, at, cols].astype(jnp.int16) & jnp.int16(plane_count - 1)
            down = down_ref[0, at, cols].astype(jnp.int16) & jnp.int16(plane_count - 1)
            bias = [None] * heads
            for t, index in enumerate((line | mask_ref[:, cols], across, down)):
                for h in range(heads):
                    found = gather_lanes(table_ref[t * heads + h], index).astype(f32)
                    bias[h] = found if t == 0 else bias[h] + found
            for h in range(heads):
                score = score_ref[h, at, cols] + bias[h]
                score_ref[h, at, cols] = score
                tops[h] = score if c == 0 else jnp.maximum(tops[h], score)
        for h in range(heads):
            top = jnp.max(tops[h], axis=1, keepdims=True)
            for c in range(keys // LANES):
                cols = slice(c * LANES, (c + 1) * LANES)
                exp_ref[h, at, cols] = jnp.exp(score_ref[h, at, cols] - top).astype(bf16)
        return carry

    lax.fori_loop(0, rows // STRIP, strip, 0)
    first = lax.broadcasted_iota(jnp.int32, (rows, LANES), 1) < HEAD
    for p in range(heads // 2):
        cols = slice(p * LANES, (p + 1) * LANES)
        even = dot_f32(exp_ref[2 * p], value_ref[2 * p])
        odd = dot_f32(exp_ref[2 * p + 1], value_ref[2 * p + 1])
        sums = jnp.where(first, pltpu.roll(even, HEAD, 1), pltpu.roll(odd, HEAD, 1))
        inverse = 1.0 / sums
        inverse_ref[:, cols] = inverse
        context_ref[:, cols] = jnp.where(first, even, odd) * inverse


def attend(query, key_wide, value_wide, buckets, mask, tables, row_count, counts):
    heads, _, keys = key_wide.shape
    width = heads * HEAD
    bucket_spec = pl.BlockSpec((1, BLOCK_ROWS, keys), lambda i: (0, i, 0))
    row_spec = pl.BlockSpec((BLOCK_ROWS, width), lambda i: (i, 0))
    return pl.pallas_call(
        partial(attend_kernel, line_count=counts[0], plane_count=counts[1]),
        grid=(row_count // BLOCK_ROWS,),
        in_specs=[
            row_spec,
            whole_spec(key_wide),
            whole_spec(value_wide),
            bucket_spec,
            bucket_spec,
            bucket_spec,
            whole_spec(mask),
            whole_spec(tables),
        ],
        out_specs=[
            pl.BlockSpec((heads, BLOCK_ROWS, keys), lambda i: (0, i, 0)),
            row_spec,
            row_spec,
        ],
        out_shape=[
            jax.ShapeDtypeStruct((heads, row_count, keys), bf16),
            jax.ShapeDtypeStruct((row_count, width), f32),
            jax.ShapeDtypeStruct((row_count, width), f32),
        ],
        scratch_shapes=[pltpu.VMEM((heads, BLOCK_ROWS, keys), f32)],
        compiler_params=pltpu.CompilerParams(vmem_limit_bytes=vmem_limit),
        name="attend",
    )(query, key_wide, value_wide, *buckets, mask, tables)


def attend_back_kernel(
    exp_ref,
    grad_ref,
    context_ref,
    query_ref,
    value_ref,
    key_ref,
    grad_score_ref,
    grad_query_ref,
    grad_key_ref,
    grad_value_ref,
):
    heads, rows, _ = exp_ref.shape

    @pl.when(pl.program_id(0) == 0)
    def _():
        grad_key_ref[...] = jnp.zeros_like(grad_key_ref)
        grad_value_ref[...] = jnp.zeros_like(grad_value_ref)

    first = lax.broadcasted_iota(jnp.int32, (rows, LANES), 1) < HEAD
    for p in range(heads // 2):
        cols = slice(p * LANES, (p + 1) * LANES)
        grad = grad_ref[:, cols]
        product = grad.astype(f32) * context_ref[:, cols]
        query_turned = query_ref[:, cols].T
        grad_turned = grad.T
        grad_query = None
        for u in range(2):
            h = 2 * p + u
            half = slice(u * HEAD, (u + 1) * HEAD)
            own = first if u == 0 else ~first
            total = jnp.sum(jnp.where(own, product, 0.0), axis=1, keepdims=True)
            grad_exp = dot_f32(grad, value_ref[h])
            grad_score = (exp_ref[h].astype(f32) * (grad_exp - total)).astype(bf16)
            grad_score_ref[h] = grad_score
            part = dot_f32(grad_score, key_ref[h])
            grad_query = part if u == 0 else grad_query + part
            grad_key_ref[h] += dot_f32(query_turned[half], grad_score)
            grad_value_ref[h] += dot_f32(grad_turned[half], exp_ref[h])
        grad_query_ref[:, cols] = (grad_query * 0.125).astype(bf16)


def attend_back(exps, grad, context, query, value_turned, key_wide):
    heads, row_count, keys = exps.shape
    width = heads * HEAD
    row_spec = pl.BlockSpec((BLOCK_ROWS, width), lambda i: (i, 0))
    exp_spec = pl.BlockSpec((heads, BLOCK_ROWS, keys), lambda i: (0, i, 0))
    sum_spec = pl.BlockSpec((heads, HEAD, keys), lambda i: (0, 0, 0))
    return pl.pallas_call(
        attend_back_kernel,
        grid=(row_count // BLOCK_ROWS,),
        in_specs=[
            exp_spec,
            row_spec,
            row_spec,
            row_spec,
            whole_spec(value_turned),
            whole_spec(key_wide),
        ],
        out_specs=[exp_spec, row_spec, sum_spec, sum_spec],
        out_shape=[
            jax.ShapeDtypeStruct((heads, row_count, keys), bf16),
            jax.ShapeDtypeStruct((row_count, width), bf16),
            jax.ShapeDtypeStruct((heads, HEAD, keys), f32),
            jax.ShapeDtypeStruct((heads, HEAD, keys), f32),
        ],
        compiler_params=pltpu.CompilerParams(vmem_limit_bytes=vmem_limit),
        name="attend_back",
    )(exps, grad, context, query, value_turned, key_wide)


def table_kernel(
    grad_score_ref, line_ref, across_ref, down_ref, out_ref, high_ref, low_ref, sum_ref, *, high_counts
):
    heads, rows, keys = grad_score_ref.shape
    step = pl.program_id(0)

    @pl.when(step == 0)
    def _():
        sum_ref[...] = jnp.zeros_like(sum_ref)

    def strip(r, carry):
        at = pl.ds(pl.multiple_of(r * STRIP, STRIP), STRIP)
        base = 0
        for t, ref in enumerate((line_ref, across_ref, down_ref)):
            for c in range(keys // LANES):
                cols = slice(c * LANES, (c + 1) * LANES)
                index = ref[0, at, cols].astype(jnp.int16)
                low = index & jnp.int16(15)
                high = index >> jnp.int16(4)
                for x in range(16):
                    low_ref[t, x * STRIP : (x + 1) * STRIP, cols] = jnp.where(
                        low == jnp.int16(x), bf16(1), bf16(0)
                    )
                for x in range(high_counts[t]):
                    mask = high == jnp.int16(x)
                    for h in range(heads):
                        start = base + (x * heads + h) * STRIP
                        high_ref[start : start + STRIP, cols] = jnp.where(
                            mask, grad_score_ref[h, at, cols], bf16(0)
                        )
            span = slice(base, base + high_counts[t] * heads * STRIP)
            sum_ref[span, :] += lax.dot_general(
                high_ref[span, :], low_ref[t], (((1,), (1,)), ((), ())), preferred_element_type=f32
            )
            base = span.stop
        return carry

    lax.fori_loop(0, rows // STRIP, strip, 0)

    @pl.when(step == pl.num_programs(0) - 1)
    def _():
        across_rows = lax.broadcasted_iota(jnp.int32, (STRIP, 16 * STRIP), 1) % STRIP
        same = across_rows == lax.broadcasted_iota(jnp.int32, (STRIP, 16 * STRIP), 0)
        for o in range(out_ref.shape[0]):
            block = sum_ref[o * STRIP : (o + 1) * STRIP, :]
            out_ref[o : o + 1, :] = jnp.sum(jnp.where(same, block, 0.0), axis=0, keepdims=True)


def table_sums(grad_scores, buckets, counts):
    heads, row_count, keys = grad_scores.shape
    high_counts = (counts[0] // 16, counts[1] // 16, counts[1] // 16)
    high_rows = sum(high_counts) * heads
    bucket_spec = pl.BlockSpec((1, BLOCK_ROWS, keys), lambda i: (0, i, 0))
    out = pl.pallas_call(
        partial(table_kernel, high_counts=high_counts),
        grid=(row_count // BLOCK_ROWS,),
        in_specs=[
            pl.BlockSpec((heads, BLOCK_ROWS, keys), lambda i: (0, i, 0)),
            bucket_spec,
            bucket_spec,
            bucket_spec,
        ],
        out_specs=pl.BlockSpec((high_rows, 16 * STRIP), lambda i: (0, 0)),
        out_shape=jax.ShapeDtypeStruct((high_rows, 16 * STRIP), f32),
        scratch_shapes=[
            pltpu.VMEM((high_rows * STRIP, keys), bf16),
            pltpu.VMEM((3, 16 * STRIP, keys), bf16),
            pltpu.VMEM((high_rows * STRIP, 16 * STRIP), f32),
        ],
        compiler_params=pltpu.CompilerParams(vmem_limit_bytes=vmem_limit),
        name="table_sums",
    )(grad_scores, *buckets)
    summed = jnp.sum(out.reshape(sum(high_counts), heads, 16, STRIP), axis=-1)
    return summed.transpose(0, 2, 1).reshape(-1, heads)


def swap(array):
    return lax.ppermute(array, "mp", [(0, 1), (1, 0)])


def both_shares(array, axis):
    other = swap(array)
    lead = lax.axis_index("mp") == 0
    return jnp.concatenate(
        [jnp.where(lead, array, other), jnp.where(lead, other, array)], axis=axis
    )


def partner(array, count, bit):
    return lax.ppermute(array, "dp", [(i, i ^ bit) for i in range(count)])


def sum_rows_over_dp(array, count):
    place = lax.axis_index("dp")
    bits = []
    bit = 1
    while bit < count:
        mine = (place // bit) % 2
        halves = array.reshape((2, array.shape[0] // 2) + array.shape[1:])
        sent = lax.dynamic_index_in_dim(halves, 1 - mine, 0, keepdims=False)
        kept = lax.dynamic_index_in_dim(halves, mine, 0, keepdims=False)
        array = kept + partner(sent, count, bit)
        bits.append(bit)
        bit *= 2
    for bit in reversed(bits):
        lead = (place // bit) % 2 == 0
        other = partner(array, count, bit)
        array = jnp.concatenate(
            [jnp.where(lead, array, other), jnp.where(lead, other, array)], axis=0
        )
    return array


def sum_small_over_dp(arrays, count):
    sizes = [a.size for a in arrays]
    total = sum(sizes)
    flat = jnp.concatenate([a.reshape(-1) for a in arrays])
    flat = jnp.pad(flat, (0, round_up(total, 1024) - total)).reshape(-1, LANES)
    bit = 1
    while bit < count:
        flat = flat + partner(flat, count, bit)
        bit *= 2
    flat = flat.reshape(-1)
    outs = []
    start = 0
    for array, size in zip(arrays, sizes):
        outs.append(flat[start : start + size].reshape(array.shape))
        start += size
    return outs


def norm_parts(values, gain_vector, shift_vector):
    average = jnp.mean(values, axis=-1, keepdims=True)
    centered = values - average
    variance = jnp.mean(centered * centered, axis=-1, keepdims=True)
    inverse = lax.rsqrt(variance + norm_epsilon)
    normal_hat = centered * inverse
    return (normal_hat * gain_vector + shift_vector, normal_hat, inverse)


def norm_back(grad_hat, normal_hat, inverse):
    first_mean = jnp.mean(grad_hat, axis=-1, keepdims=True)
    cross_mean = jnp.mean(grad_hat * normal_hat, axis=-1, keepdims=True)
    return inverse * (grad_hat - first_mean - normal_hat * cross_mean)


def widen(heads_rows, other):
    fill = jnp.full(heads_rows[:, 0].shape, other, bf16)
    wide = []
    for h in range(heads_rows.shape[1]):
        parts = [heads_rows[:, h], fill]
        wide.append(jnp.concatenate(parts if h % 2 == 0 else parts[::-1], axis=1))
    return jnp.stack(wide)


def per_device(
    dp_count,
    tokens,
    cotangent,
    long_flag,
    token_mask,
    bucket_line,
    bucket_across,
    bucket_down,
    project_weight,
    project_bias,
    table_line,
    table_across,
    table_down,
    output_weight,
    output_bias,
    first_gain,
    first_shift,
    expand_weight,
    expand_bias,
    reduce_weight,
    reduce_bias,
    second_gain,
    second_shift,
):
    length = tokens.shape[1]
    width = project_weight.shape[2]
    heads = table_line.shape[1]
    counts = (table_line.shape[0], table_across.shape[0])
    rows = round_up(length, BLOCK_ROWS)
    keys = round_up(length, LANES)
    buckets = (bucket_line, bucket_across, bucket_down)
    mp_index = lax.axis_index("mp")

    positions = jnp.arange(length, dtype=jnp.int32)
    limit = jnp.where(long_flag[0] > 0, LONG, SHORT).astype(jnp.int32)
    valid = ((token_mask[0] > 0) & (positions < limit)).astype(f32)
    valid_rows = jnp.pad(valid, (0, rows - length))[:, None]
    valid_keys = jnp.pad(valid, (0, keys - length))
    mask = jnp.broadcast_to(
        jnp.where(valid_keys > 0, 0, counts[0]).astype(jnp.int16), (STRIP, keys)
    )
    tables = []
    for table in (table_line, table_across, table_down):
        lanes = jnp.pad(
            table.T, ((0, 0), (0, LANES - table.shape[0])), constant_values=large_negative
        )
        tables.append(jnp.broadcast_to(lanes[:, None, :], (heads, STRIP, LANES)))
    tables = jnp.concatenate(tables).astype(bf16)

    output_full = both_shares(output_weight, 0)
    padded = jnp.pad(tokens[0], ((0, keys - length), (0, 0)))
    token_rows = padded[:rows]
    projected = jnp.einsum("ld,kde->kle", padded, project_weight, preferred_element_type=f32)
    query = (projected[0] + project_bias[0].astype(f32)).astype(bf16) * bf16(0.125)
    key_heads = projected[1].astype(bf16).reshape(keys, heads, HEAD)
    value_heads = (projected[2] + project_bias[1].astype(f32)).astype(bf16)
    value_heads = value_heads.reshape(keys, heads, HEAD)
    key_wide = widen(key_heads, 0)
    value_ones = widen(value_heads, 1)
    value_wide = widen(value_heads, 0)

    exps, context, inverse = attend(
        query,
        key_wide.transpose(0, 2, 1),
        value_ones,
        buckets,
        mask,
        tables,
        rows,
        counts,
    )
    context_low = context.astype(bf16)
    context_full = both_shares(context_low, 1)
    attended = dot_f32(context_full, output_full) + output_bias.astype(f32)
    first_norm, first_hat, first_inverse = norm_parts(
        token_rows.astype(f32) + attended, first_gain, first_shift
    )
    expand_input = first_norm.astype(bf16)
    before = dot_f32(expand_input, expand_weight) + expand_bias.astype(f32)
    activated, gelu_back = jax.vjp(partial(jax.nn.gelu, approximate=False), before)
    activated_low = activated.astype(bf16)
    reduced_part = dot_f32(activated_low, reduce_weight).astype(bf16)
    reduced = reduced_part.astype(f32) + swap(reduced_part).astype(f32)
    reduced = reduced + reduce_bias.astype(f32)
    second_norm, second_hat, second_inverse = norm_parts(
        first_norm + reduced, second_gain, second_shift
    )
    layer_out = (second_norm * valid_rows).astype(bf16)[None, :length]
    grad_out = jnp.pad(cotangent[0], ((0, rows - length), (0, 0))).astype(f32) * valid_rows
    second_gain_grad = jnp.sum(grad_out * second_hat, axis=0)
    second_shift_grad = jnp.sum(grad_out, axis=0)
    grad_mixed = norm_back(grad_out * second_gain, second_hat, second_inverse)
    grad_reduced = grad_mixed.astype(bf16)
    reduce_bias_grad = jnp.sum(grad_reduced, axis=0, dtype=f32)
    reduce_weight_grad = jnp.einsum(
        "lf,ld->fd", activated_low, grad_reduced, preferred_element_type=f32
    )
    grad_active = jnp.einsum("ld,fd->lf", grad_reduced, reduce_weight, preferred_element_type=f32)
    grad_before = gelu_back(grad_active)[0].astype(bf16)
    expand_bias_grad = jnp.sum(grad_before, axis=0, dtype=f32)
    expand_weight_grad = jnp.einsum(
        "ld,lf->df", expand_input, grad_before, preferred_element_type=f32
    )
    reduce_weight_grad = sum_rows_over_dp(reduce_weight_grad.astype(bf16), dp_count)
    expand_weight_grad = sum_rows_over_dp(expand_weight_grad.astype(bf16), dp_count)

    hidden_part = jnp.einsum(
        "lf,df->ld", grad_before, expand_weight, preferred_element_type=f32
    ).astype(bf16)
    hidden = hidden_part.astype(f32) + swap(hidden_part).astype(f32)
    grad_first = grad_mixed + hidden
    first_gain_grad = jnp.sum(grad_first * first_hat, axis=0)
    first_shift_grad = jnp.sum(grad_first, axis=0)
    grad_inner = norm_back(grad_first * first_gain, first_hat, first_inverse)
    grad_attended = grad_inner.astype(bf16)
    output_bias_grad = jnp.sum(grad_attended, axis=0, dtype=f32)
    output_weight_grad = jnp.einsum(
        "le,lf->ef", context_low, grad_attended, preferred_element_type=f32
    )
    output_weight_grad = sum_rows_over_dp(output_weight_grad.astype(bf16), dp_count)
    grad_context = jnp.einsum(
        "lf,ef->le", grad_attended, output_weight, preferred_element_type=f32
    )
    grad_scaled = (grad_context * inverse).astype(bf16)

    grad_scores, grad_query, grad_key, grad_value = attend_back(
        exps, grad_scaled, context, query, value_wide.transpose(0, 2, 1), key_wide
    )
    grad_key = grad_key.reshape(width, keys)[:, :rows].astype(bf16)
    grad_value = grad_value.reshape(width, keys)[:, :rows].astype(bf16)
    project_weight_grad = jnp.stack(
        [
            jnp.einsum("ld,le->de", token_rows, grad_query, preferred_element_type=f32),
            jnp.einsum("ld,el->de", token_rows, grad_key, preferred_element_type=f32),
            jnp.einsum("ld,el->de", token_rows, grad_value, preferred_element_type=f32),
        ]
    ).astype(bf16)
    project_weight_grad = sum_rows_over_dp(
        project_weight_grad.reshape(-1, width), dp_count
    ).reshape(project_weight.shape)
    project_bias_grad = jnp.stack(
        [jnp.sum(grad_query, axis=0, dtype=f32), jnp.sum(grad_value, axis=1, dtype=f32)]
    )
    input_part = (
        jnp.einsum("le,de->ld", grad_query, project_weight[0], preferred_element_type=f32)
        + jnp.einsum("el,de->ld", grad_key, project_weight[1], preferred_element_type=f32)
        + jnp.einsum("el,de->ld", grad_value, project_weight[2], preferred_element_type=f32)
    )
    lead = mp_index == 0
    sent = jnp.where(lead, input_part[:, width:], input_part[:, :width]).astype(bf16)
    own = jnp.where(
        lead,
        input_part[:, :width] + grad_inner[:, :width],
        input_part[:, width:] + grad_inner[:, width:],
    )
    input_grad = (own + swap(sent).astype(f32))[None, :length]

    table_grads = table_sums(grad_scores, buckets, counts)
    (
        second_gain_grad,
        second_shift_grad,
        reduce_bias_grad,
        expand_bias_grad,
        first_gain_grad,
        first_shift_grad,
        output_bias_grad,
    ) = sum_small_over_dp(
        [
            second_gain_grad,
            second_shift_grad,
            reduce_bias_grad,
            expand_bias_grad,
            first_gain_grad,
            first_shift_grad,
            output_bias_grad,
        ],
        dp_count,
    )
    table_grads, project_bias_grad = sum_small_over_dp([table_grads, project_bias_grad], dp_count)
    mine = mp_index * width
    return (
        layer_out,
        input_grad,
        project_weight_grad.astype(f32),
        project_bias_grad,
        table_grads[: counts[0]],
        table_grads[counts[0] : counts[0] + counts[1]],
        table_grads[counts[0] + counts[1] :],
        output_weight_grad.astype(f32),
        output_bias_grad,
        lax.dynamic_slice_in_dim(first_gain_grad, mine, width, 0),
        lax.dynamic_slice_in_dim(first_shift_grad, mine, width, 0),
        expand_weight_grad.astype(f32),
        expand_bias_grad,
        reduce_weight_grad.astype(f32),
        reduce_bias_grad,
        second_gain_grad,
        second_shift_grad,
    )


def solution(mesh):
    placed = (
        P("dp", None, None),
        P("dp", None, None),
        P("dp"),
        P("dp", None),
        P("dp", None, None),
        P("dp", None, None),
        P("dp", None, None),
        P(None, None, "mp"),
        P(None, "mp"),
        P(None, "mp"),
        P(None, "mp"),
        P(None, "mp"),
        P("mp", None),
        P(),
        P(),
        P(),
        P(None, "mp"),
        P("mp"),
        P("mp", None),
        P(),
        P(),
        P(),
    )
    return jax.shard_map(
        partial(per_device, mesh.shape["dp"]),
        mesh=mesh,
        in_specs=placed,
        out_specs=(
            P("dp", None, None),
            P("dp", None, "mp"),
            P(None, None, "mp"),
            P(None, "mp"),
            P(None, "mp"),
            P(None, "mp"),
            P(None, "mp"),
            P("mp", None),
            P(),
            P("mp"),
            P("mp"),
            P(None, "mp"),
            P("mp"),
            P("mp", None),
            P(),
            P(),
            P(),
        ),
        check_vma=False,
    )
```

time: 1280 us -> 566 us (0.44)
  matrix products: 462 us -> 64.8 us
  local copies, waits for them, and re-layouts: 386 us -> 88 us
  Pallas kernels: 0 us -> 149 us
  waiting for transfers between devices: 258 us -> 153 us
  blocking collectives: 67.1 us -> 0 us
  starting transfers between devices: 0.25 us -> 54.3 us
  loops' own time: 18.7 us -> 0 us
  other arithmetic: 64.3 us -> 49.4 us
  between operations: 15.9 us -> 2.85 us
    dot_general x36 -> x16, matrix products: 462 us -> 64.8 us  [the longest x3 25 us: dot_f32(): return jnp.dot(left, right, preferred_element_type=f32)]
    dynamic_update_slice x6 -> x0, local copies, waits for them, and re-layouts: 208 us -> none  [fill(): return lax.dynamic_update_slice_in_dim(position_bias, summed, row_start, 2)]
    psum x3 -> x0, waiting for transfers between devices: 184 us -> none  [the longest x1 93.3 us: heads_layer(): attended = lax.psum(attended_part, 'mp') + output_bias.astype(jnp.float32)]
    ppermute x0 -> x45, waiting for transfers between devices: none -> 153 us  [the longest x5 84.7 us: swap(): return lax.ppermute(array, 'mp', [(0, 1), (1, 0)])]
    pallas_call x0 -> x3, Pallas kernels: none -> 149 us  [the longest x1 78.3 us: table_sums(): pl.pallas_call(partial(table_kernel, high_counts=high_counts), grid=(row_...]
    dynamic_slice x34 -> x2, local copies, waits for them, and re-layouts: 101 us -> 1.3 us  [the longest x1 0.65 us: per_device(): lax.dynamic_slice_in_dim(first_shift_grad, mine, width, 0)]
    psum x2 -> x0, blocking collectives: 67.1 us -> none  [the longest x1 62 us: final_total(): lax.psum((project_weight_grad, project_bias_grad, table_line_grad, table_...]
    ppermute x0 -> x45, starting transfers between devices: none -> 54.3 us  [the longest x40 49.1 us: partner(): return lax.ppermute(array, 'dp', [(i, i ^ bit) for i in range(count)])]
  transfers between devices with their start and end apart: 6 -> 45, of which waited for: 4 -> 23; matrix products, arithmetic and copies ran while one was open for 21% -> 24% of each run, Pallas kernels for 0% -> 27%
where the time goes in v1:
time: 566 us; the launch traced here: 562 us
  waiting for transfers between devices  153 us (27%)
  Pallas kernels  149 us (26%)
  local copies, waits for them, and re-layouts  88 us (16%)
  matrix products  64.8 us (11%)
  starting transfers between devices  54.3 us (10%)
  other arithmetic  49.4 us (9%)
    ppermute x5, waiting for transfers between devices, swap(): return lax.ppermute(array, 'mp', [(0, 1), (1, 0)])  84.7 us
    pallas_call x1, Pallas kernels, table_sums(): pl.pallas_call(partial(table_kernel, high_counts=high_counts), grid=(row_...  78.3 us
    ppermute x40, waiting for transfers between devices, partner(): return lax.ppermute(array, 'dp', [(i, i ^ bit) for i in range(count)])  68.1 us
    unnamed x141, local copies, waits for them, and re-layouts  52.8 us
    ppermute x40, starting transfers between devices, partner(): return lax.ppermute(array, 'dp', [(i, i ^ bit) for i in range(count)])  49.1 us
    pallas_call x1, Pallas kernels, attend(): pl.pallas_call(partial(attend_kernel, line_count=counts[0], plane_count=c...  48.1 us
    dot_general x3, matrix products, dot_f32(): return jnp.dot(left, right, preferred_element_type=f32)  25 us
    pallas_call x1, Pallas kernels, attend_back(): pl.pallas_call(attend_back_kernel, grid=(row_count // BLOCK_ROWS,), in_sp...  22.9 us
  transfers between devices with their start and end apart: 45, of which 23 were waited for; matrix products, arithmetic and copies ran while one was open for 24% of the time, Pallas kernels for 27%

profile of v1, /device:TPU:0, one launch (start us, length us, event | category | flops | bytes accessed | tf_op | source)
XLA Modules:
  0.0 561.5 jit_solution(2068564581135920818)
XLA Ops:
  3.7 4.5 convolution_bitcast_fusion
  55.3 3.8 copy.83.key_ref
  59.1 3.8 copy.84.value_ref
  63.6 48.1 %attend.1 = (bf16[6,1120,1152]{2,1,0:T(8,128)(2,1)}, f32[1120,384]{1,0:T(8,128)}, f32[1120,384]{1,0:T(8,128)}) custom-call(bf16[1152,384]{1,0:T(8,128)(2,1)} %fusion.32.query_ref, bf16[6,128,1152]{2,1,0:T(8,128)(2,1)} %copy.83.key_ref, bf16[6,1152,128]{2,1,0:T(8,128)(2,1)} %copy.84.value_ref, s32[1,1089,1089]{2,1,0:T(8,128)} %copy.85.line_ref, ...), custom_call_target="tpu_custom_call" | custom-call | tf_op jit(solution)/shard_map/attend/pallas_call | solution.py:117
  115.0 19.0 %collective-permute-done = bf16[1120,384]{1,0:T(8,128)(2,1)} collective-permute-done((bf16[1120,384]{1,0:T(8,128)(2,1)S(1)}, bf16[1120,384]{1,0:T(8,128)(2,1)}, u32[]{:S(2)}, u32[]{:S(2)}) %collective-permute-start) | collective-permute-done | bytes 860192 | tf_op jit(solution)/shard_map/ppermute | solution.py:294
  137.8 19.2 %multiply_convert_fusion = (bf16[1120,1536]{1,0:T(8,128)(2,1)S(1)}, f32[1120,1536]{1,0:T(8,128)}, f32[1120,1536]{1,0:T(8,128)}) fusion(f32[1536]{0:T(1024)S(1)} %convert_element_type.155, bf16[768,1536]{1,0:T(8,128)(2,1)S(1)} %copy-done, f32[1120,768]{1,0:T(8,128)S(1)} %get-tuple-element.175, f32[768]{0:T(1024)S(1)} %copy-done.34, f32[768]{0:T(1024)S(1)} %copy-done.29, ...), kind=kOutput, calls=%fused_computation.5 | convolution fusion | flops 2760253440 | bytes 23024384 | tf_op jit(solution)/shard_map/dot_general | solution.py:34
  157.0 4.1 convolution_convert_fusion.3
  161.7 37.9 %collective-permute-done.2 = bf16[1120,768]{1,0:T(8,128)(2,1)} collective-permute-done((bf16[1120,768]{1,0:T(8,128)(2,1)}, bf16[1120,768]{1,0:T(8,128)(2,1)}, u32[]{:S(2)}, u32[]{:S(2)}) %collective-permute-start.2) | collective-permute-done | bytes 1720352 | tf_op jit(solution)/shard_map/ppermute | solution.py:294
  199.6 4.4 fusion.62
  209.9 3.6 convolution_convert_fusion
  213.5 9.2 %convert_reduce_fusion = (f32[1536]{0:T(1024)S(1)}, bf16[1120,1536]{1,0:T(8,128)(2,1)}) fusion(f32[1120,1536]{1,0:T(8,128)} %get-tuple-element.101, f32[1120,1536]{1,0:T(8,128)} %get-tuple-element.176, bf16[1536,768]{1,0:T(8,128)(2,1)S(1)} %copy-done.43, f32[1120,768]{1,0:T(8,128)S(1)} %get-tuple-element.95), kind=kOutput, calls=%fused_computation.3 | convolution fusion | flops 2670795264 | bytes 23009280 | tf_op jit(solution)/shard_map/ld,fd->lf/dot_general | solution.py:470
  222.7 5.0 convolution_convert_fusion.2
  227.7 4.0 convolution_convert_fusion.1
  244.3 27.8 %collective-permute-done.3 = bf16[1120,768]{1,0:T(8,128)(2,1)S(1)} collective-permute-done((bf16[1120,768]{1,0:T(8,128)(2,1)S(1)}, bf16[1120,768]{1,0:T(8,128)(2,1)S(1)}, u32[]{:S(2)}, u32[]{:S(2)}) %collective-permute-start.3) | collective-permute-done | bytes 1720352 | tf_op jit(solution)/shard_map/ppermute | solution.py:294
  279.4 22.9 %attend_back.1 = (bf16[6,1120,1152]{2,1,0:T(8,128)(2,1)}, bf16[1120,384]{1,0:T(8,128)(2,1)}, f32[6,64,1152]{2,1,0:T(8,128)}, f32[6,64,1152]{2,1,0:T(8,128)}) custom-call(bf16[6,1120,1152]{2,1,0:T(8,128)(2,1)} %get-tuple-element.25.exp_ref, bf16[1120,384]{1,0:T(8,128)(2,1)} %fusion.14.grad_ref, f32[1120,384]{1,0:T(8,128)} %get-tuple-element.24.context_ref, ...), custom_call_target="tpu_custom_call" | custom-call | tf_op jit(solution)/shard_map/attend_back/pallas_call | solution.py:194
  321.3 78.3 %table_sums.1 = f32[60,256]{1,0:T(8,128)} custom-call(bf16[6,1120,1152]{2,1,0:T(8,128)(2,1)} %get-tuple-element.30.grad_score_ref, s32[1,1089,1089]{2,1,0:T(8,128)} %copy.85.line_ref, s32[1,1089,1089]{2,1,0:T(8,128)} %copy.86.across_ref, s32[1,1089,1089]{2,1,0:T(8,128)} %copy.87.down_ref), custom_call_target="tpu_custom_call" | custom-call | tf_op jit(solution)/shard_map/table_sums/pallas_call | solution.py:270
  435.2 3.9 collective-permute-done.27
  465.4 3.8 collective-permute-done.20
  487.6 6.0 %copy.92 = f32[1,1089,384]{2,0,1:T(1,128)} copy(f32[1,1089,384]{2,1,0:T(8,128)S(1)} %fusion.24) | data formatting | bytes 3345408
  497.4 10.6 %collective-permute-done.6 = bf16[576,384]{1,0:T(8,128)(2,1)S(1)} collective-permute-done((bf16[576,384]{1,0:T(8,128)(2,1)S(1)}, bf16[576,384]{1,0:T(8,128)(2,1)S(1)}, u32[]{:S(2)}, u32[]{:S(2)}) %collective-permute-start.6) | collective-permute-done | bytes 442400 | tf_op jit(solution)/shard_map/ppermute | solution.py:306
  518.8 3.8 collective-permute-done.8
  524.5 8.4 %collective-permute-done.35 = bf16[192,1536]{1,0:T(8,128)(2,1)S(1)} collective-permute-done((bf16[192,1536]{1,0:T(8,128)(2,1)S(1)}, bf16[192,1536]{1,0:T(8,128)(2,1)S(1)}, u32[]{:S(2)}, u32[]{:S(2)}) %collective-permute-start.35) | collective-permute-done | bytes 589856 | tf_op jit(solution)/shard_map/ppermute | solution.py:306
  535.5 5.1 collective-permute-done.10
  543.7 8.4 %collective-permute-done.11 = bf16[576,384]{1,0:T(8,128)(2,1)S(1)} collective-permute-done((bf16[576,384]{1,0:T(8,128)(2,1)S(1)}, bf16[576,384]{1,0:T(8,128)(2,1)S(1)}, u32[]{:S(2)}, u32[]{:S(2)}) %collective-permute-start.11) | collective-permute-done | bytes 442400 | tf_op jit(solution)/shard_map/ppermute | solution.py:306
  (381 shorter events, 213.0 us)
Async XLA Ops:
  0.7 112.8 %collective-permute-start.1 = (bf16[384,768]{1,0:T(8,128)(2,1)}, bf16[384,768]{1,0:T(8,128)(2,1)}, u32[]{:S(2)}, u32[]{:S(2)}) collective-permute-start(bf16[384,768]{1,0:T(8,128)(2,1)} %param.34), channel_id=1, source_target_pairs={{0,1},{1,0},{2,3},{3,2},{4,5},{5,4},{6,7},{7,6},{8,9},{9,8},{10,11... | collective-permute-start | bytes 1769480 | tf_op jit(solution)/shard_map/ppermute | solution.py:294
  113.2 20.8 %collective-permute-start = (bf16[1120,384]{1,0:T(8,128)(2,1)S(1)}, bf16[1120,384]{1,0:T(8,128)(2,1)}, u32[]{:S(2)}, u32[]{:S(2)}) collective-permute-start(bf16[1120,384]{1,0:T(8,128)(2,1)S(1)} %convert_element_type.152), channel_id=1, source_target_pairs={{0,1},{1,0},{2,3},{3,2},{4,5},{5,4},{6,7},{7,6},{8,9},{9,8},{10,11... | collective-permute-start | bytes 2580488 | tf_op jit(solution)/shard_map/ppermute | solution.py:294
  161.1 38.4 %collective-permute-start.2 = (bf16[1120,768]{1,0:T(8,128)(2,1)}, bf16[1120,768]{1,0:T(8,128)(2,1)}, u32[]{:S(2)}, u32[]{:S(2)}) collective-permute-start(bf16[1120,768]{1,0:T(8,128)(2,1)} %convolution_convert_fusion.3), channel_id=1, source_target_pairs={{0,1},{1,0},{2,3},{3,2},{4,5},{5,4},{6,7},{7,6},{8,9},{9,8},{10,11... | collective-permute-start | bytes 5160968 | tf_op jit(solution)/shard_map/ppermute | solution.py:294
  232.0 10.6 %collective-permute-start.29 = (bf16[384,1536]{1,0:T(8,128)(2,1)S(1)}, bf16[384,1536]{1,0:T(8,128)(2,1)S(1)}, u32[]{:S(2)}, u32[]{:S(2)}) collective-permute-start(bf16[384,1536]{1,0:T(8,128)(2,1)S(1)} %dynamic-slice_bitcast_fusion.1), channel_id=1, source_target_pairs={{0,2},{2,0},{4,6},{6,4},{8,10},{10,8},{12,14},{14,12},{16,18},{18,... | collective-permute-start | bytes 3538952 | tf_op jit(solution)/shard_map/ppermute | solution.py:306
  232.6 39.5 %collective-permute-start.3 = (bf16[1120,768]{1,0:T(8,128)(2,1)S(1)}, bf16[1120,768]{1,0:T(8,128)(2,1)S(1)}, u32[]{:S(2)}, u32[]{:S(2)}) collective-permute-start(bf16[1120,768]{1,0:T(8,128)(2,1)S(1)} %convolution_convert_fusion.2), channel_id=1, source_target_pairs={{0,1},{1,0},{2,3},{3,2},{4,5},{5,4},{6,7},{7,6},{8,9},{9,8},{10,11... | collective-permute-start | bytes 5160968 | tf_op jit(solution)/shard_map/ppermute | solution.py:294
  241.2 186.0 %collective-permute-start.38 = (bf16[384,768]{1,0:T(8,128)(2,1)}, bf16[384,768]{1,0:T(8,128)(2,1)}, u32[]{:S(2)}, u32[]{:S(2)}) collective-permute-start(bf16[384,768]{1,0:T(8,128)(2,1)} %dynamic-slice_bitcast_fusion.3), channel_id=1, source_target_pairs={{0,4},{2,6},{4,0},{6,2},{8,12},{10,14},{12,8},{14,10},{16,20},{18,... | collective-permute-start | bytes 1769480 | tf_op jit(solution)/shard_map/ppermute | solution.py:306
  243.7 189.9 %collective-permute-start.30 = (bf16[192,1536]{1,0:T(8,128)(2,1)}, bf16[192,1536]{1,0:T(8,128)(2,1)}, u32[]{:S(2)}, u32[]{:S(2)}) collective-permute-start(bf16[192,1536]{1,0:T(8,128)(2,1)} %dynamic-slice_bitcast_fusion.4), channel_id=1, source_target_pairs={{0,4},{2,6},{4,0},{6,2},{8,12},{10,14},{12,8},{14,10},{16,20},{18,... | collective-permute-start | bytes 1769480 | tf_op jit(solution)/shard_map/ppermute | solution.py:306
  403.5 10.4 %collective-permute-start.25 = (f32[48,128]{1,0:T(8,128)}, f32[48,128]{1,0:T(8,128)}, u32[]{:S(2)}, u32[]{:S(2)}) collective-permute-start(f32[48,128]{1,0:T(8,128)} %bitcast.81), channel_id=1, source_target_pairs={{0,2},{2,0},{4,6},{6,4},{8,10},{10,8},{12,14},{14,12},{16,18},{18,... | collective-permute-start | bytes 73736 | tf_op jit(solution)/shard_map/ppermute | solution.py:306
  406.4 41.8 %collective-permute-start.17 = (bf16[192,768]{1,0:T(8,128)(2,1)}, bf16[192,768]{1,0:T(8,128)(2,1)}, u32[]{:S(2)}, u32[]{:S(2)}) collective-permute-start(bf16[192,768]{1,0:T(8,128)(2,1)} %dynamic-slice_bitcast_fusion.8), channel_id=1, source_target_pairs={{0,2},{2,0},{4,6},{6,4},{8,10},{10,8},{12,14},{14,12},{16,18},{18,... | collective-permute-start | bytes 884744 | tf_op jit(solution)/shard_map/ppermute | solution.py:306
  414.0 79.7 %collective-permute-start.5 = (bf16[1152,384]{1,0:T(8,128)(2,1)}, bf16[1152,384]{1,0:T(8,128)(2,1)}, u32[]{:S(2)}, u32[]{:S(2)}) collective-permute-start(bf16[1152,384]{1,0:T(8,128)(2,1)} %dynamic-slice_bitcast_fusion.2), channel_id=1, source_target_pairs={{0,2},{2,0},{4,6},{6,4},{8,10},{10,8},{12,14},{14,12},{16,18},{18,... | collective-permute-start | bytes 2654216 | tf_op jit(solution)/shard_map/ppermute | solution.py:306
  418.6 67.5 %collective-permute-start.4 = (bf16[1120,384]{1,0:T(8,128)(2,1)}, bf16[1120,384]{1,0:T(8,128)(2,1)}, u32[]{:S(2)}, u32[]{:S(2)}) collective-permute-start(bf16[1120,384]{1,0:T(8,128)(2,1)} %select_convert_fusion), channel_id=1, source_target_pairs={{0,1},{1,0},{2,3},{3,2},{4,5},{5,4},{6,7},{7,6},{8,9},{9,8},{10,11... | collective-permute-start | bytes 2580488 | tf_op jit(solution)/shard_map/ppermute | solution.py:294
  431.3 19.6 %collective-permute-start.39 = (bf16[192,768]{1,0:T(8,128)(2,1)S(1)}, bf16[192,768]{1,0:T(8,128)(2,1)S(1)}, u32[]{:S(2)}, u32[]{:S(2)}) collective-permute-start(bf16[192,768]{1,0:T(8,128)(2,1)S(1)} %dynamic-slice_bitcast_fusion.6), channel_id=1, source_target_pairs={{0,8},{2,10},{4,12},{6,14},{8,0},{10,2},{12,4},{14,6},{16,24},{18,... | collective-permute-start | bytes 884744 | tf_op jit(solution)/shard_map/ppermute | solution.py:306
  450.9 14.4 %collective-permute-start.40 = (bf16[96,768]{1,0:T(8,128)(2,1)S(1)}, bf16[96,768]{1,0:T(8,128)(2,1)S(1)}, u32[]{:S(2)}, u32[]{:S(2)}) collective-permute-start(bf16[96,768]{1,0:T(8,128)(2,1)S(1)} %dynamic-slice_bitcast_fusion.10), channel_id=1, source_target_pairs={{0,16},{2,18},{4,20},{6,22},{8,24},{10,26},{12,28},{14,30},{16,0},... | collective-permute-start | bytes 442376 | tf_op jit(solution)/shard_map/ppermute | solution.py:306
  454.9 14.3 %collective-permute-start.32 = (bf16[48,1536]{1,0:T(8,128)(2,1)S(1)}, bf16[48,1536]{1,0:T(8,128)(2,1)S(1)}, u32[]{:S(2)}, u32[]{:S(2)}) collective-permute-start(bf16[48,1536]{1,0:T(8,128)(2,1)S(1)} %dynamic-slice_bitcast_fusion.11), channel_id=1, source_target_pairs={{0,16},{2,18},{4,20},{6,22},{8,24},{10,26},{12,28},{14,30},{16,0},... | collective-permute-start | bytes 442376 | tf_op jit(solution)/shard_map/ppermute | solution.py:306
  465.3 11.9 %collective-permute-start.41 = (bf16[96,768]{1,0:T(8,128)(2,1)S(1)}, bf16[96,768]{1,0:T(8,128)(2,1)S(1)}, u32[]{:S(2)}, u32[]{:S(2)}) collective-permute-start(bf16[96,768]{1,0:T(8,128)(2,1)S(1)} %bitcast_add_fusion.10), channel_id=1, source_target_pairs={{0,16},{2,18},{4,20},{6,22},{8,24},{10,26},{12,28},{14,30},{16,0},... | collective-permute-start | bytes 442376 | tf_op jit(solution)/shard_map/ppermute | solution.py:306
  477.3 19.3 %collective-permute-start.42 = (bf16[192,768]{1,0:T(8,128)(2,1)S(1)}, bf16[192,768]{1,0:T(8,128)(2,1)S(1)}, u32[]{:S(2)}, u32[]{:S(2)}) collective-permute-start(bf16[192,768]{1,0:T(8,128)(2,1)S(1)} %pad_maximum_fusion.10), channel_id=1, source_target_pairs={{0,8},{2,10},{4,12},{6,14},{8,0},{10,2},{12,4},{14,6},{16,24},{18,... | collective-permute-start | bytes 884744 | tf_op jit(solution)/shard_map/ppermute | solution.py:306
  482.3 15.0 %collective-permute-start.34 = (bf16[96,1536]{1,0:T(8,128)(2,1)S(1)}, bf16[96,1536]{1,0:T(8,128)(2,1)S(1)}, u32[]{:S(2)}, u32[]{:S(2)}) collective-permute-start(bf16[96,1536]{1,0:T(8,128)(2,1)S(1)} %pad_maximum_fusion.9), channel_id=1, source_target_pairs={{0,8},{2,10},{4,12},{6,14},{8,0},{10,2},{12,4},{14,6},{16,24},{18,... | collective-permute-start | bytes 884744 | tf_op jit(solution)/shard_map/ppermute | solution.py:306
  486.0 32.6 %collective-permute-start.24 = (bf16[192,768]{1,0:T(8,128)(2,1)S(1)}, bf16[192,768]{1,0:T(8,128)(2,1)S(1)}, u32[]{:S(2)}, u32[]{:S(2)}) collective-permute-start(bf16[192,768]{1,0:T(8,128)(2,1)S(1)} %pad_maximum_fusion.8), channel_id=1, source_target_pairs={{0,2},{2,0},{4,6},{6,4},{8,10},{10,8},{12,14},{14,12},{16,18},{18,... | collective-permute-start | bytes 884744 | tf_op jit(solution)/shard_map/ppermute | solution.py:306
  495.0 13.0 %collective-permute-start.6 = (bf16[576,384]{1,0:T(8,128)(2,1)S(1)}, bf16[576,384]{1,0:T(8,128)(2,1)S(1)}, u32[]{:S(2)}, u32[]{:S(2)}) collective-permute-start(bf16[576,384]{1,0:T(8,128)(2,1)S(1)} %dynamic-slice_bitcast_fusion.5), channel_id=1, source_target_pairs={{0,4},{2,6},{4,0},{6,2},{8,12},{10,14},{12,8},{14,10},{16,20},{18,... | collective-permute-start | bytes 1327112 | tf_op jit(solution)/shard_map/ppermute | solution.py:306
  496.7 45.5 %collective-permute-start.43 = (bf16[384,768]{1,0:T(8,128)(2,1)S(1)}, bf16[384,768]{1,0:T(8,128)(2,1)S(1)}, u32[]{:S(2)}, u32[]{:S(2)}) collective-permute-start(bf16[384,768]{1,0:T(8,128)(2,1)S(1)} %pad_maximum_fusion.6), channel_id=1, source_target_pairs={{0,4},{2,6},{4,0},{6,2},{8,12},{10,14},{12,8},{14,10},{16,20},{18,... | collective-permute-start | bytes 1769480 | tf_op jit(solution)/shard_map/ppermute | solution.py:306
  510.4 22.5 %collective-permute-start.35 = (bf16[192,1536]{1,0:T(8,128)(2,1)S(1)}, bf16[192,1536]{1,0:T(8,128)(2,1)S(1)}, u32[]{:S(2)}, u32[]{:S(2)}) collective-permute-start(bf16[192,1536]{1,0:T(8,128)(2,1)S(1)} %pad_maximum_fusion.5), channel_id=1, source_target_pairs={{0,4},{2,6},{4,0},{6,2},{8,12},{10,14},{12,8},{14,10},{16,20},{18,... | collective-permute-start | bytes 1769480 | tf_op jit(solution)/shard_map/ppermute | solution.py:306
  522.6 10.5 %collective-permute-start.9 = (bf16[144,384]{1,0:T(8,128)(2,1)S(1)}, bf16[144,384]{1,0:T(8,128)(2,1)S(1)}, u32[]{:S(2)}, u32[]{:S(2)}) collective-permute-start(bf16[144,384]{1,0:T(8,128)(2,1)S(1)} %bitcast_add_fusion.13), channel_id=1, source_target_pairs={{0,16},{2,18},{4,20},{6,22},{8,24},{10,26},{12,28},{14,30},{16,0},... | collective-permute-start | bytes 331784 | tf_op jit(solution)/shard_map/ppermute | solution.py:306
  535.5 17.0 %collective-permute-start.36 = (bf16[384,1536]{1,0:T(8,128)(2,1)S(1)}, bf16[384,1536]{1,0:T(8,128)(2,1)S(1)}, u32[]{:S(2)}, u32[]{:S(2)}) collective-permute-start(bf16[384,1536]{1,0:T(8,128)(2,1)S(1)} %pad_maximum_fusion.2), channel_id=1, source_target_pairs={{0,2},{2,0},{4,6},{6,4},{8,10},{10,8},{12,14},{14,12},{16,18},{18,... | collective-permute-start | bytes 3538952 | tf_op jit(solution)/shard_map/ppermute | solution.py:306
  540.8 11.3 %collective-permute-start.11 = (bf16[576,384]{1,0:T(8,128)(2,1)S(1)}, bf16[576,384]{1,0:T(8,128)(2,1)S(1)}, u32[]{:S(2)}, u32[]{:S(2)}) collective-permute-start(bf16[576,384]{1,0:T(8,128)(2,1)S(1)} %pad_maximum_fusion.7), channel_id=1, source_target_pairs={{0,4},{2,6},{4,0},{6,2},{8,12},{10,14},{12,8},{14,10},{16,20},{18,... | collective-permute-start | bytes 1327112 | tf_op jit(solution)/shard_map/ppermute | solution.py:306
  (77 other events, 870.3 us)
